TPU v7x, 32 devices: a whole 2x2x4 slice. The times are simulated.
32 devices in a mesh: gx: 8 (over z, core), gy: 4 (over y, x).
Axes of the slice: x: 2, y: 2, z: 4, core: 2. Of those that a mesh axis runs over, the one named last changes fastest.
Arguments:
- density: float32 [128, 32, 128], P('gx', 'gy'), may hold values from 0.05 to 0.95
- displacement: float32 [3, 128, 32, 128], P(None, 'gx', 'gy'), may hold values from -2 to 2
- passive: int32 [128, 32, 128], P('gx', 'gy'), may hold values from 0 to 2
Outputs:
- new_density: float32 [128, 32, 128], P('gx', 'gy')
- sensitivity: float32 [128, 32, 128], P('gx', 'gy')
All inputs are finite; a program needn't handle non-finite values.
Results may differ from a plain program's by a relative error of at most 0.0003.
Values sent between devices are 32-bit elements; how exact they have to be, the bound alone decides.
A program may use at most 64 MiB of HBM per device.

v0:
```python
import functools
import math

import jax
import jax.numpy as jnp
from jax import lax
from jax.experimental import pallas as pl
from jax.experimental.pallas import tpu as pltpu
from jax.sharding import PartitionSpec as P

BISECT = 8
BRACKET = 8.0
MOVE_LIMIT = 0.2
VOLUME_SHARE = 0.35
DERIVATIVE = 3.0 * (1.0 - 1e-09)
EDGE_WEIGHT = 1.5 - math.sqrt(2.0)
POISSON = 0.3
LAME_FIRST = POISSON / ((1.0 + POISSON) * (1.0 - 2.0 * POISSON))
SHEAR = 0.5 / (1.0 + POISSON)
ROWS = 8
MESH = pl.DeviceIdType.MESH
WAYS = [(1, 0), (-1, 0), (0, 1), (0, -1), (1, 1), (-1, 1), (1, -1), (-1, -1)]


def z_neighbours(value, lane):
    planes = value.shape[-1]
    axis = value.ndim - 1
    above = jnp.where(lane == planes - 1, 0.0, pltpu.roll(value, planes - 1, axis))
    below = jnp.where(lane == 0, 0.0, pltpu.roll(value, 1, axis))
    return above + below


def parts_of_filter(value, lane):
    beside = z_neighbours(value, lane)
    return (
        1.5 * value + 0.5 * beside,
        0.5 * value + EDGE_WEIGHT * beside,
        EDGE_WEIGHT * value,
    )


def filter_rows(packed, lane, cols_x):
    _, near, far = parts_of_filter(packed, lane)
    count = packed.shape[0]
    return (near + pltpu.roll(far, 1, 0) + pltpu.roll(far, count - 1, 0))[:cols_x]


def filter_chunk(field, first, size, row_low, row_high, row, lane):
    planes = field.shape[-1]
    value = field[pl.ds(first * ROWS, (size + 2) * ROWS), :].reshape(size + 2, ROWS, planes)
    own, near, far = parts_of_filter(value, lane)
    side = near[1:-1] + far[:-2] + far[2:]
    above = row_high[pl.ds(first * ROWS, size * ROWS), :].reshape(size, ROWS, planes)
    below = row_low[pl.ds(first * ROWS, size * ROWS), :].reshape(size, ROWS, planes)
    above = jnp.where(row == ROWS - 1, above, pltpu.roll(side, ROWS - 1, 1))
    below = jnp.where(row == 0, below, pltpu.roll(side, 1, 1))
    return own[1:-1] + near[:-2] + near[2:] + (above + below)


def corner_modes(value, row_high, row, lane):
    planes = value.shape[-1]
    above = jnp.where(row == ROWS - 1, row_high, pltpu.roll(value, ROWS - 1, 1))
    total, step = value + above, above - value

    def next_z(field):
        return jnp.where(lane == planes - 1, 0.0, pltpu.roll(field, planes - 1, 2))

    total_next, step_next = next_z(total), next_z(step)
    both = total + total_next
    along_z = total_next - total
    along_y = step + step_next
    along_yz = step_next - step
    return (
        both[1:] - both[:-1],
        along_y[1:] + along_y[:-1],
        along_z[1:] + along_z[:-1],
        along_y[1:] - along_y[:-1],
        along_z[1:] - along_z[:-1],
        along_yz[1:] + along_yz[:-1],
        along_yz[1:] - along_yz[:-1],
    )


def element_energy(modes):
    (ax, ay, az, axy, axz, ayz, axyz), (bx, by, bz, bxy, bxz, byz, bxyz), (
        cx,
        cy,
        cz,
        cxy,
        cxz,
        cyz,
        cxyz,
    ) = modes

    def sq(value):
        return value * value

    first = (
        (LAME_FIRST / 16.0) * sq(ax + by + cz)
        + (2.0 * SHEAR / 16.0) * (sq(ax) + sq(by) + sq(cz))
        + (SHEAR / 16.0) * (sq(ay + bx) + sq(az + cx) + sq(bz + cy))
    )
    second = (
        (LAME_FIRST / 48.0) * (sq(axy + cyz) + sq(bxy + cxz) + sq(axz + byz))
        + (3.0 * SHEAR / 48.0) * (sq(axy) + sq(axz) + sq(bxy) + sq(byz) + sq(cxz) + sq(cyz))
        + (SHEAR / 48.0) * (sq(ayz + bxz) + sq(ayz + cxy) + sq(bxz + cxy))
    )
    third = ((LAME_FIRST + 4.0 * SHEAR) / 144.0) * (sq(axyz) + sq(bxyz) + sq(cxyz))
    return first + second + third


def peers(count, body):
    if count <= 64:
        for step in range(1, count):
            body(step)
    else:
        lax.fori_loop(1, count, lambda step, carry: (body(step), carry)[1], 0)


def kernel(
    count_x,
    count_y,
    dens_hbm,
    disp_hbm,
    pas_hbm,
    results,
    big,
    passive,
    pack_low,
    pack_high,
    row_high,
    row_low,
    spread,
    spread_pack_low,
    spread_pack_high,
    spread_row_high,
    spread_row_low,
    corner_pp,
    corner_mp,
    corner_pm,
    corner_mm,
    s_corner_pp,
    s_corner_mp,
    s_corner_pm,
    s_corner_mm,
    node_row,
    tail_high,
    tail_low,
    inverse,
    inverse_volume,
    scaled,
    lower,
    upper,
    sum_scaled,
    sum_lower,
    sum_upper,
    partial,
    totals,
    local_sems,
    send_a,
    recv_a,
    send_b,
    recv_b,
    send_c,
    recv_c,
):
    new_out, sens_out = results.at[0], results.at[1]
    planes = dens_hbm.shape[-1]
    cols_x = dens_hbm.shape[0] // ROWS
    block = cols_x * ROWS
    last = cols_x * ROWS
    ix, iy = lax.axis_index("gx"), lax.axis_index("gy")
    total_x, total_y = cols_x * count_x, ROWS * count_y

    def inside(x, y):
        return (x >= 0) & (x < count_x) & (y >= 0) & (y < count_y)

    loads = [
        pltpu.make_async_copy(dens_hbm, big.at[0, pl.ds(ROWS, block)], local_sems.at[0]),
        pltpu.make_async_copy(disp_hbm, big.at[pl.ds(1, 3), pl.ds(ROWS, block)], local_sems.at[1]),
        pltpu.make_async_copy(pas_hbm, passive, local_sems.at[2]),
    ]
    for load in loads:
        load.start()

    devices = count_x * count_y

    def peer(step):
        return (lax.rem(ix + step // count_y, count_x), lax.rem(iy + step % count_y, count_y))

    barrier = pltpu.get_barrier_semaphore()
    peers(
        devices,
        lambda step: pl.semaphore_signal(
            barrier, inc=1, device_id=peer(step), device_id_type=MESH
        ),
    )

    def fill(way, refs):
        @pl.when(jnp.logical_not(inside(ix - way[0], iy - way[1])))
        def _():
            for ref in refs:
                ref[...] = jnp.zeros(ref.shape, ref.dtype)

    def exchange(pairs, send, recv):
        def copy(at):
            source, target = pairs[at]
            dx, dy = WAYS[at]
            return pltpu.make_async_remote_copy(
                src_ref=source,
                dst_ref=target,
                send_sem=send.at[at],
                recv_sem=recv.at[at],
                device_id=(ix + dx, iy + dy),
                device_id_type=MESH,
            )

        def start(at):
            dx, dy = WAYS[at]

            @pl.when(inside(ix + dx, iy + dy))
            def _():
                copy(at).start()

        def arrive(at):
            dx, dy = WAYS[at]

            @pl.when(inside(ix - dx, iy - dy))
            def _():
                copy(at).wait_recv()

        def sent(at):
            dx, dy = WAYS[at]

            @pl.when(inside(ix + dx, iy + dy))
            def _():
                copy(at).wait_send()

        return start, arrive, sent

    first_tile, last_tile = pl.ds(ROWS, ROWS), pl.ds(last, ROWS)
    low_tile, high_tile = pl.ds(0, ROWS), pl.ds(last + ROWS, ROWS)
    start_a, arrive_a, sent_a = exchange(
        [
            (big.at[0, last_tile], big.at[0, low_tile]),
            (big.at[:, first_tile], big.at[:, high_tile]),
            (pack_high, row_low.at[pl.ds(0, cols_x)]),
            (pack_low, row_high.at[:, pl.ds(0, cols_x)]),
            (big.at[0, last_tile], corner_pp),
            (big.at[0, first_tile], corner_mp),
            (big.at[0, last_tile], corner_pm),
            (big.at[:, first_tile], corner_mm),
        ],
        send_a,
        recv_a,
    )
    start_b, arrive_b, sent_b = exchange(
        [
            (spread.at[last_tile], spread.at[low_tile]),
            (spread.at[first_tile], spread.at[high_tile]),
            (spread_pack_high, spread_row_low.at[pl.ds(0, cols_x)]),
            (spread_pack_low, spread_row_high.at[pl.ds(0, cols_x)]),
            (spread.at[last_tile], s_corner_pp),
            (spread.at[first_tile], s_corner_mp),
            (spread.at[last_tile], s_corner_pm),
            (spread.at[first_tile], s_corner_mm),
        ],
        send_b,
        recv_b,
    )
    fill(WAYS[0], [big.at[0, low_tile], spread.at[low_tile]])
    fill(WAYS[1], [big.at[:, high_tile], spread.at[high_tile]])
    fill(WAYS[2], [row_low.at[pl.ds(0, cols_x)], spread_row_low.at[pl.ds(0, cols_x)]])
    fill(WAYS[3], [row_high.at[:, pl.ds(0, cols_x)], spread_row_high.at[pl.ds(0, cols_x)]])
    fill(WAYS[4], [corner_pp, s_corner_pp])
    fill(WAYS[5], [corner_mp, s_corner_mp])
    fill(WAYS[6], [corner_pm, s_corner_pm])
    fill(WAYS[7], [corner_mm, s_corner_mm])

    def strided(start):
        return pl.ds(start, cols_x, stride=ROWS)

    loads[0].wait()
    pack_high[...] = big[0, strided(ROWS + ROWS - 1), :]
    pack_low[0] = big[0, strided(ROWS), :]
    loads[1].wait()
    for c in (1, 2, 3):
        pack_low[c] = big[c, strided(ROWS), :]
    pl.semaphore_wait(barrier, devices - 1)
    for at in (3, 1, 2, 7, 0, 4, 5, 6):
        start_a(at)

    lane = lax.broadcasted_iota(jnp.int32, (ROWS, planes), 1)
    row = lax.broadcasted_iota(jnp.int32, (ROWS, planes), 0)

    def counted(at, total):
        one, none = jnp.float32(1.0), jnp.float32(0.0)
        return jnp.where(at > 0, one, none) + jnp.where(at < total - 1, one, none)

    count_z = counted(lane, planes)
    known = {}

    def representative(x):
        return x if x in (-1, 0, cols_x - 1, cols_x) else 1

    def inverse_sums(x, offset):
        x = representative(x)
        if (x, offset) not in known:
            y = iy * ROWS + row + offset
            beside_y = counted(y, total_y)
            global_x = ix * cols_x + x
            beside_x = counted(global_x, total_x)
            sums = (
                1.5
                + 0.5 * (beside_x + beside_y + count_z)
                + EDGE_WEIGHT * (beside_x * beside_y + beside_x * count_z + beside_y * count_z)
            )
            result = 1.0 / sums
            result = jnp.where((y >= 0) & (y < total_y), result, 0.0)
            if x in (-1, cols_x):
                held = (global_x >= 0) & (global_x < total_x)
                result = result * jnp.where(held, jnp.float32(1.0), jnp.float32(0.0))
            known[x, offset] = (result, parts_of_filter(result, lane))
        return known[x, offset]

    weights = {}
    for x in range(cols_x):
        tile = pl.ds(x * ROWS, ROWS)
        inverse[tile, :] = inverse_sums(x, 0)[0]
        key = tuple(representative(x + d) for d in (-1, 0, 1))
        if key not in weights:
            volume = inverse_sums(x, 0)[1][0]
            volume = volume + inverse_sums(x - 1, 0)[1][1] + inverse_sums(x + 1, 0)[1][1]
            for offset in (-1, 1):
                volume = volume + inverse_sums(x, offset)[1][1]
                volume = volume + inverse_sums(x - 1, offset)[1][2]
                volume = volume + inverse_sums(x + 1, offset)[1][2]
            weights[key] = 1.0 / volume
        inverse_volume[tile, :] = weights[key]

    def masks(size):
        shape = (size, ROWS, planes)
        return (
            lax.broadcasted_iota(jnp.int32, shape, 1),
            lax.broadcasted_iota(jnp.int32, shape, 2),
        )

    size = 4 if cols_x % 4 == 0 else 1
    rows_here = size * ROWS
    row_s, lane_s = masks(size)
    row_1, lane_1 = masks(size + 1)
    _, lane_2 = masks(size + 2)

    def tiles(ref, first):
        return ref[pl.ds(first * ROWS, rows_here), :].reshape(size, ROWS, planes)

    loads[2].wait()
    for first in range(0, cols_x, size):
        at = pl.ds(first * ROWS, rows_here)
        kind = tiles(passive, first)
        held = big[0, pl.ds((first + 1) * ROWS, rows_here), :].reshape(size, ROWS, planes)
        fixed = jnp.where(kind == 1, 1.0, 0.0)
        low = jnp.where(kind == 0, jnp.maximum(held - MOVE_LIMIT, 0.0), fixed)
        high = jnp.where(kind == 0, jnp.minimum(held + MOVE_LIMIT, 1.0), fixed)
        lower[at, :] = low.reshape(rows_here, planes)
        upper[at, :] = high.reshape(rows_here, planes)

    for at in range(8):
        arrive_a(at)

    def join(rows, first, final):
        rows[pl.ds(cols_x, ROWS), :] = jnp.where(row == 0, first, jnp.where(row == 7, final, 0.0))

    def tails(rows_high, rows_low, pp, mp, pm, mm):
        join(rows_high, mm[0:1, :], pm[0:1, :])
        join(rows_low, mp[7:8, :], pp[7:8, :])
        lane_rows = lax.broadcasted_iota(jnp.int32, (cols_x + ROWS, planes), 1)
        tail_high[strided(ROWS - 1), :] = filter_rows(rows_high[...], lane_rows, cols_x)
        tail_low[strided(0), :] = filter_rows(rows_low[...], lane_rows, cols_x)

    tails(row_high.at[0], row_low, corner_pp, corner_mp, corner_pm, corner_mm.at[0])
    for c in range(3):
        node_row[c, strided(ROWS - 1), :] = row_high[1 + c, pl.ds(0, cols_x), :]
        node_row[c, pl.ds(block + ROWS - 1, 1), :] = corner_mm[1 + c, 0:1, :]

    density = big.at[0]

    for first in range(0, cols_x, size):
        near = pl.ds((first + 1) * ROWS, (size + 1) * ROWS)
        high = pl.ds(first * ROWS, (size + 1) * ROWS)
        shape = (size + 1, ROWS, planes)
        modes = [
            corner_modes(
                big[1 + c, near, :].reshape(shape),
                node_row[c, high, :].reshape(shape),
                row_1,
                lane_1,
            )
            for c in range(3)
        ]
        energy = element_energy(modes)
        inv = tiles(inverse, first)
        kind = tiles(passive, first)
        physical = filter_chunk(density, first, size, tail_low, tail_high, row_s, lane_2) * inv
        physical = jnp.where(kind == 1, 1.0, jnp.where(kind == 2, 0.0, physical))
        raw = (-DERIVATIVE) * physical * physical * energy
        spread[pl.ds((first + 1) * ROWS, rows_here), :] = (raw * inv).reshape(rows_here, planes)

    spread_pack_high[...] = spread[strided(ROWS + ROWS - 1), :]
    spread_pack_low[...] = spread[strided(ROWS), :]
    for at in (3, 2, 1, 0, 7, 4, 5, 6):
        start_b(at)

    def rate_of(sens, held, weight):
        return held * jnp.sqrt(-sens * weight)

    def middle_rows(value, index):
        return jnp.where((index > 0) & (index < ROWS - 1), value, 0.0)

    def plane_group(first, count, place):
        shape = (count, ROWS, planes)
        row_c = lax.broadcasted_iota(jnp.int32, shape, 1)
        lane_c = lax.broadcasted_iota(jnp.int32, (count + 2, ROWS, planes), 2)
        wide = spread[pl.ds(first * ROWS, (count + 2) * ROWS), :].reshape(count + 2, ROWS, planes)
        own, near, far = parts_of_filter(wide, lane_c)
        side = near[1:-1] + far[:-2] + far[2:]
        sens = own[1:-1] + near[:-2] + near[2:]
        sens = sens + (pltpu.roll(side, ROWS - 1, 1) + pltpu.roll(side, 1, 1))
        at = pl.ds(first * ROWS, count * ROWS)
        held = big[0, pl.ds((first + 1) * ROWS, count * ROWS), :].reshape(shape)
        sens = middle_rows(sens, row_c)
        rate = rate_of(sens, held, inverse_volume[at, :].reshape(shape))
        sens_out[at, :] = sens.reshape(count * ROWS, planes)
        scaled[at, :] = rate.reshape(count * ROWS, planes)
        to = pl.ds(place * ROWS, count * ROWS)
        sum_scaled[to, :] = rate.reshape(count * ROWS, planes)
        for source, target in ((lower, sum_lower), (upper, sum_upper)):
            kept = middle_rows(source[at, :].reshape(shape), row_c)
            target[to, :] = kept.reshape(count * ROWS, planes)

    slots = 2**BISECT
    group = 16
    spacing = 2.0 * BRACKET / slots
    scales = jnp.concatenate(
        [jnp.full((1, ROWS, planes), math.exp(-0.5 * spacing * j), jnp.float32) for j in range(group)]
    )

    def add_volumes(first_tile, end_tile, fresh):
        def volumes(i, carry):
            begin = (-BRACKET) + (spacing * group) * i.astype(jnp.float32)
            factors = scales * jnp.exp(jnp.full((ROWS, planes), -0.5 * begin, jnp.float32))[None]
            at = pl.ds(pl.multiple_of(i * (group * ROWS), group * ROWS), group * ROWS)
            if fresh:
                total = jnp.zeros((group, ROWS, planes), jnp.float32)
            else:
                total = partial[at, :].reshape(group, ROWS, planes)
            for x in range(first_tile, end_tile):
                tile = pl.ds(x * ROWS, ROWS)
                moved = jnp.maximum(sum_scaled[tile, :][None] * factors, sum_lower[tile, :][None])
                total = total + jnp.minimum(moved, sum_upper[tile, :][None])
            partial[at, :] = total.reshape(group * ROWS, planes)
            return carry

        lax.fori_loop(0, slots // group, volumes, 0)

    inner = cols_x - 2
    for first in range(1, 1 + inner, size):
        plane_group(first, min(size, 1 + inner - first), first - 1)
    add_volumes(0, inner, True)

    for at in range(8):
        arrive_b(at)
    plane_group(0, 1, inner)
    plane_group(cols_x - 1, 1, inner + 1)
    join(spread_row_high, s_corner_mm[0:1, :], s_corner_pm[0:1, :])
    join(spread_row_low, s_corner_mp[7:8, :], s_corner_pp[7:8, :])
    lane_p = lax.broadcasted_iota(jnp.int32, (cols_x + ROWS, planes), 1)

    def packed_row(r):
        above = spread[pl.ds(last + ROWS + r, 1), :]
        below = spread[pl.ds(r, 1), :]
        tail = jnp.where(row == 0, above, jnp.where(row == ROWS - 1, below, 0.0))
        return jnp.concatenate([spread[strided(ROWS + r), :], tail], axis=0)

    def edge_row(r, beyond, next_row, held, place):
        own, near, _ = parts_of_filter(packed_row(r), lane_p)
        count = own.shape[0]
        sens = (own + pltpu.roll(near, 1, 0) + pltpu.roll(near, count - 1, 0))[:cols_x]
        sens = sens + filter_rows(beyond, lane_p, cols_x)
        sens = sens + filter_rows(packed_row(next_row), lane_p, cols_x)
        rate = rate_of(sens, held, inverse_volume[strided(r), :])
        sens_out[strided(r), :] = sens
        scaled[strided(r), :] = rate
        to = pl.ds(place * ROWS, cols_x)
        sum_scaled[to, :] = rate
        sum_lower[to, :] = lower[strided(r), :]
        sum_upper[to, :] = upper[strided(r), :]

    edge_row(0, spread_row_low[...], 1, pack_low[0], inner + 2)
    edge_row(ROWS - 1, spread_row_high[...], ROWS - 2, pack_high[...], inner + 2 + cols_x // ROWS)
    add_volumes(inner, inner + 2 + 2 * (cols_x // ROWS), False)
    me = ix * count_y + iy
    halves = slots // planes
    for half in range(halves):
        start = half * planes * ROWS
        lines = partial[pl.ds(start, planes, stride=ROWS), :]
        for s in range(1, ROWS):
            lines = lines + partial[pl.ds(start + s, planes, stride=ROWS), :]
        totals[me, half : half + 1, :] = jnp.sum(lines.T, axis=0, keepdims=True)

    def share(step):
        pltpu.make_async_remote_copy(
            src_ref=totals.at[me],
            dst_ref=totals.at[me],
            send_sem=send_c,
            recv_sem=recv_c,
            device_id=peer(step),
            device_id_type=MESH,
        ).start()

    peers(devices, share)
    others = totals.at[pl.ds(0, devices - 1)]
    pltpu.make_async_copy(others, others, recv_c).wait()
    volume = jnp.sum(totals[...], axis=0)
    label = lax.broadcasted_iota(jnp.int32, volume.shape, 0) * planes + lax.broadcasted_iota(
        jnp.int32, volume.shape, 1
    )
    target = VOLUME_SHARE * total_x * total_y * planes
    over = jnp.where((label > 0) & (volume > target), 1.0, 0.0)
    reached = jnp.sum(jnp.sum(over, axis=0, keepdims=True), axis=1, keepdims=True)
    middle = (-BRACKET) + spacing * (jnp.broadcast_to(reached, (ROWS, planes)) + 0.5)
    factor = jnp.exp(-0.5 * middle)[None]
    for first in range(0, cols_x, size):
        at = pl.ds(first * ROWS, rows_here)
        moved = jnp.maximum(tiles(scaled, first) * factor, tiles(lower, first))
        new_out[at, :] = jnp.minimum(moved, tiles(upper, first)).reshape(rows_here, planes)
    for at in range(8):
        sent_a(at)
        sent_b(at)
    pltpu.make_async_copy(others, others, send_c).wait()


def per_device(count_x, count_y, density, displacement, passive):
    cols_x, cols_y, planes = density.shape
    assert cols_y == ROWS and cols_x % ROWS == 0 and planes == 128
    block = cols_x * ROWS
    slots = 2**BISECT

    def buffer(*shape):
        return pltpu.VMEM(shape, jnp.float32)

    field = buffer(block, planes)
    tile = buffer(ROWS, planes)
    wide = buffer(block + 2 * ROWS, planes)
    rows = buffer(cols_x, planes)
    sums = buffer(block + 2 * cols_x, planes)
    ring = buffer(cols_x + ROWS, planes)
    held = functools.partial(pltpu.with_memory_space_constraint, memory_space=pltpu.HBM)
    anywhere = pl.BlockSpec(memory_space=pl.ANY)
    out = jax.ShapeDtypeStruct((2, block, planes), jnp.float32)
    results = pl.pallas_call(
        functools.partial(kernel, count_x, count_y),
        out_shape=out,
        in_specs=[anywhere] * 3,
        out_specs=pl.BlockSpec(memory_space=pltpu.VMEM),
        scratch_shapes=[
            buffer(4, block + 2 * ROWS, planes),
            pltpu.VMEM((block, planes), jnp.int32),
            buffer(4, cols_x, planes),
            rows,
            buffer(4, cols_x + ROWS, planes),
            ring,
            wide,
            rows,
            rows,
            ring,
            ring,
            tile,
            tile,
            tile,
            buffer(4, ROWS, planes),
            tile,
            tile,
            tile,
            tile,
            buffer(3, block + ROWS, planes),
            field,
            field,
            field,
            field,
            field,
            field,
            field,
            sums,
            sums,
            sums,
            buffer(slots * ROWS, planes),
            buffer(count_x * count_y, slots // planes, planes),
            pltpu.SemaphoreType.DMA((3,)),
            pltpu.SemaphoreType.DMA((8,)),
            pltpu.SemaphoreType.DMA((8,)),
            pltpu.SemaphoreType.DMA((8,)),
            pltpu.SemaphoreType.DMA((8,)),
            pltpu.SemaphoreType.DMA,
            pltpu.SemaphoreType.DMA,
        ],
        compiler_params=pltpu.CompilerParams(
            collective_id=0, has_side_effects=True, vmem_limit_bytes=16 * 1024 * 1024
        ),
    )(
        held(density.reshape(block, planes)),
        held(displacement.reshape(3, block, planes)),
        held(passive.reshape(block, planes)),
    )
    return (results[0].reshape(density.shape), results[1].reshape(density.shape))


def solution(mesh):
    return jax.shard_map(
        functools.partial(per_device, mesh.shape["gx"], mesh.shape["gy"]),
        mesh=mesh,
        in_specs=(P("gx", "gy", None), P(None, "gx", "gy", None), P("gx", "gy", None)),
        out_specs=(P("gx", "gy", None), P("gx", "gy", None)),
        check_vma=False,
    )
```

profile of v0, /device:TPU:0, one launch (start us, length us, event | category | flops | bytes accessed | tf_op | source)
XLA Modules:
  0.0 20.5 jit_solution(3030856454961330292)
XLA Ops:
  0.6 19.2 %shard_map.50 = f32[2,128,128]{2,1,0:T(8,128)S(1)} custom-call(f32[128,128]{1,0:T(8,128)} %bitcast.8, f32[3,128,128]{2,1,0:T(8,128)} %bitcast.7, s32[128,128]{1,0:T(8,128)} %bitcast.9), custom_call_target="tpu_custom_call" | custom-call | tf_op jit(solution)/shard_map/pallas_call | solution.py:561
  19.8 0.7 %slice_bitcast_fusion = (f32[16,8,128]{2,1,0:T(8,128)}, f32[16,8,128]{2,1,0:T(8,128)}) fusion(f32[2,128,128]{2,1,0:T(8,128)S(1)} %shard_map.50), kind=kLoop, calls=%fused_computation | loop fusion | bytes 262144 | tf_op jit(solution)/shard_map/reshape;squeeze | solution.py:615
where the time goes:
time: 20.6 us; the launch traced here: 20.5 us
  Pallas kernels  19.2 us (93%)
  local copies, waits for them, and re-layouts  0.66 us (3%)
  between operations  0.64 us (3%)
    pallas_call x1, Pallas kernels, per_device(): pl.pallas_call(functools.partial(kernel, count_x, count_y), out_shape=out...  19.2 us
    another operation x1, local copies, waits for them, and re-layouts, per_device(): results[1].reshape(density.shape)  0.66 us

commit v1 on v0

--- a/solution.py
+++ b/solution.py
@@ -45,39 +45,47 @@
     return (near + pltpu.roll(far, 1, 0) + pltpu.roll(far, count - 1, 0))[:cols_x]
 
 
-def filter_chunk(field, first, size, row_low, row_high, row, lane):
-    planes = field.shape[-1]
-    value = field[pl.ds(first * ROWS, (size + 2) * ROWS), :].reshape(size + 2, ROWS, planes)
-    own, near, far = parts_of_filter(value, lane)
+def packed_filter(beyond, here, beyond_next, lane, cols_x):
+    own, near, _ = parts_of_filter(here, lane)
+    count = here.shape[0]
+    result = (own + pltpu.roll(near, 1, 0) + pltpu.roll(near, count - 1, 0))[:cols_x]
+    result = result + filter_rows(beyond, lane, cols_x)
+    return result + filter_rows(beyond_next, lane, cols_x)
+
+
+def plane_filter(wide, lane):
+    own, near, far = parts_of_filter(wide, lane)
     side = near[1:-1] + far[:-2] + far[2:]
-    above = row_high[pl.ds(first * ROWS, size * ROWS), :].reshape(size, ROWS, planes)
-    below = row_low[pl.ds(first * ROWS, size * ROWS), :].reshape(size, ROWS, planes)
-    above = jnp.where(row == ROWS - 1, above, pltpu.roll(side, ROWS - 1, 1))
-    below = jnp.where(row == 0, below, pltpu.roll(side, 1, 1))
-    return own[1:-1] + near[:-2] + near[2:] + (above + below)
-
-
-def corner_modes(value, row_high, row, lane):
+    result = own[1:-1] + near[:-2] + near[2:]
+    return result + (pltpu.roll(side, ROWS - 1, 1) + pltpu.roll(side, 1, 1))
+
+
+def corner_modes(value, above, lane, packed):
     planes = value.shape[-1]
-    above = jnp.where(row == ROWS - 1, row_high, pltpu.roll(value, ROWS - 1, 1))
     total, step = value + above, above - value
 
     def next_z(field):
-        return jnp.where(lane == planes - 1, 0.0, pltpu.roll(field, planes - 1, 2))
+        moved = pltpu.roll(field, planes - 1, field.ndim - 1)
+        return jnp.where(lane == planes - 1, 0.0, moved)
+
+    def ends(field):
+        if packed:
+            return field, pltpu.roll(field, field.shape[0] - 1, 0)
+        return field[:-1], field[1:]
 
     total_next, step_next = next_z(total), next_z(step)
-    both = total + total_next
-    along_z = total_next - total
-    along_y = step + step_next
-    along_yz = step_next - step
+    both, both_next = ends(total + total_next)
+    along_z, along_z_next = ends(total_next - total)
+    along_y, along_y_next = ends(step + step_next)
+    along_yz, along_yz_next = ends(step_next - step)
     return (
-        both[1:] - both[:-1],
-        along_y[1:] + along_y[:-1],
-        along_z[1:] + along_z[:-1],
-        along_y[1:] - along_y[:-1],
-        along_z[1:] - along_z[:-1],
-        along_yz[1:] + along_yz[:-1],
-        along_yz[1:] - along_yz[:-1],
+        both_next - both,
+        along_y_next + along_y,
+        along_z_next + along_z,
+        along_y_next - along_y,
+        along_z_next - along_z,
+        along_yz_next + along_yz,
+        along_yz_next - along_yz,
     )
 
 
@@ -143,9 +151,6 @@
     s_corner_mp,
     s_corner_pm,
     s_corner_mm,
-    node_row,
-    tail_high,
-    tail_low,
     inverse,
     inverse_volume,
     scaled,
@@ -268,15 +273,6 @@
         send_b,
         recv_b,
     )
-    fill(WAYS[0], [big.at[0, low_tile], spread.at[low_tile]])
-    fill(WAYS[1], [big.at[:, high_tile], spread.at[high_tile]])
-    fill(WAYS[2], [row_low.at[pl.ds(0, cols_x)], spread_row_low.at[pl.ds(0, cols_x)]])
-    fill(WAYS[3], [row_high.at[:, pl.ds(0, cols_x)], spread_row_high.at[pl.ds(0, cols_x)]])
-    fill(WAYS[4], [corner_pp, s_corner_pp])
-    fill(WAYS[5], [corner_mp, s_corner_mp])
-    fill(WAYS[6], [corner_pm, s_corner_pm])
-    fill(WAYS[7], [corner_mm, s_corner_mm])
-
     def strided(start):
         return pl.ds(start, cols_x, stride=ROWS)
 
@@ -289,6 +285,14 @@
     pl.semaphore_wait(barrier, devices - 1)
     for at in (3, 1, 2, 7, 0, 4, 5, 6):
         start_a(at)
+    fill(WAYS[0], [big.at[0, low_tile], spread.at[low_tile]])
+    fill(WAYS[1], [big.at[:, high_tile], spread.at[high_tile]])
+    fill(WAYS[2], [row_low.at[pl.ds(0, cols_x)], spread_row_low.at[pl.ds(0, cols_x)]])
+    fill(WAYS[3], [row_high.at[:, pl.ds(0, cols_x)], spread_row_high.at[pl.ds(0, cols_x)]])
+    fill(WAYS[4], [corner_pp, s_corner_pp])
+    fill(WAYS[5], [corner_mp, s_corner_mp])
+    fill(WAYS[6], [corner_pm, s_corner_pm])
+    fill(WAYS[7], [corner_mm, s_corner_mm])
 
     lane = lax.broadcasted_iota(jnp.int32, (ROWS, planes), 1)
     row = lax.broadcasted_iota(jnp.int32, (ROWS, planes), 0)
@@ -338,19 +342,8 @@
             weights[key] = 1.0 / volume
         inverse_volume[tile, :] = weights[key]
 
-    def masks(size):
-        shape = (size, ROWS, planes)
-        return (
-            lax.broadcasted_iota(jnp.int32, shape, 1),
-            lax.broadcasted_iota(jnp.int32, shape, 2),
-        )
-
     size = 4 if cols_x % 4 == 0 else 1
     rows_here = size * ROWS
-    row_s, lane_s = masks(size)
-    row_1, lane_1 = masks(size + 1)
-    _, lane_2 = masks(size + 2)
-
     def tiles(ref, first):
         return ref[pl.ds(first * ROWS, rows_here), :].reshape(size, ROWS, planes)
 
@@ -365,49 +358,78 @@
         lower[at, :] = low.reshape(rows_here, planes)
         upper[at, :] = high.reshape(rows_here, planes)
 
+    def spread_of(density_sum, modes, kind, inv):
+        physical = density_sum * inv
+        physical = jnp.where(kind == 1, 1.0, jnp.where(kind == 2, 0.0, physical))
+        raw = (-DERIVATIVE) * physical * physical * element_energy(modes)
+        return raw * inv
+
+    def spread_planes(first, count):
+        shape = (count, ROWS, planes)
+        lane_c = lax.broadcasted_iota(jnp.int32, (count + 2, ROWS, planes), 2)
+        wide = big[0, pl.ds(first * ROWS, (count + 2) * ROWS), :]
+        density_sum = plane_filter(wide.reshape(count + 2, ROWS, planes), lane_c)
+        modes = []
+        for c in range(3):
+            value = big[1 + c, pl.ds((first + 1) * ROWS, (count + 1) * ROWS), :]
+            value = value.reshape(count + 1, ROWS, planes)
+            modes.append(corner_modes(value, pltpu.roll(value, ROWS - 1, 1), lane_c[:-1], False))
+        at = pl.ds(first * ROWS, count * ROWS)
+        result = spread_of(
+            density_sum, modes, passive[at, :].reshape(shape), inverse[at, :].reshape(shape)
+        )
+        to = pl.ds((first + 1) * ROWS, count * ROWS)
+        spread[to, :] = result.reshape(count * ROWS, planes)
+
+    inner = cols_x - 2
+    for first in range(1, 1 + inner, size):
+        spread_planes(first, min(size, 1 + inner - first))
+
     for at in range(8):
         arrive_a(at)
 
     def join(rows, first, final):
-        rows[pl.ds(cols_x, ROWS), :] = jnp.where(row == 0, first, jnp.where(row == 7, final, 0.0))
-
-    def tails(rows_high, rows_low, pp, mp, pm, mm):
-        join(rows_high, mm[0:1, :], pm[0:1, :])
-        join(rows_low, mp[7:8, :], pp[7:8, :])
-        lane_rows = lax.broadcasted_iota(jnp.int32, (cols_x + ROWS, planes), 1)
-        tail_high[strided(ROWS - 1), :] = filter_rows(rows_high[...], lane_rows, cols_x)
-        tail_low[strided(0), :] = filter_rows(rows_low[...], lane_rows, cols_x)
-
-    tails(row_high.at[0], row_low, corner_pp, corner_mp, corner_pm, corner_mm.at[0])
-    for c in range(3):
-        node_row[c, strided(ROWS - 1), :] = row_high[1 + c, pl.ds(0, cols_x), :]
-        node_row[c, pl.ds(block + ROWS - 1, 1), :] = corner_mm[1 + c, 0:1, :]
-
+        rows[pl.ds(cols_x, ROWS), :] = jnp.where(
+            row == 0, first, jnp.where(row == ROWS - 1, final, 0.0)
+        )
+
+    lane_p = lax.broadcasted_iota(jnp.int32, (cols_x + ROWS, planes), 1)
+
+    def packed_row(field, r):
+        above = field[pl.ds(last + ROWS + r, 1), :]
+        below = field[pl.ds(r, 1), :]
+        tail = jnp.where(row == 0, above, jnp.where(row == ROWS - 1, below, 0.0))
+        return jnp.concatenate([field[strided(ROWS + r), :], tail], axis=0)
+
+    def packed_nodes(c, r):
+        above = big[c, pl.ds(last + ROWS + r, 1), :]
+        tail = jnp.where(row == 0, above, 0.0)
+        return jnp.concatenate([big[c, strided(ROWS + r), :], tail], axis=0)
+
+    spread_planes(0, 1)
+    spread_planes(cols_x - 1, 1)
+    join(row_high.at[0], corner_mm[0, 0:1, :], corner_pm[0:1, :])
+    join(row_low, corner_mp[ROWS - 1 : ROWS, :], corner_pp[ROWS - 1 : ROWS, :])
+    for c in (1, 2, 3):
+        join(row_high.at[c], corner_mm[c, 0:1, :], 0.0)
     density = big.at[0]
 
-    for first in range(0, cols_x, size):
-        near = pl.ds((first + 1) * ROWS, (size + 1) * ROWS)
-        high = pl.ds(first * ROWS, (size + 1) * ROWS)
-        shape = (size + 1, ROWS, planes)
-        modes = [
-            corner_modes(
-                big[1 + c, near, :].reshape(shape),
-                node_row[c, high, :].reshape(shape),
-                row_1,
-                lane_1,
-            )
-            for c in range(3)
-        ]
-        energy = element_energy(modes)
-        inv = tiles(inverse, first)
-        kind = tiles(passive, first)
-        physical = filter_chunk(density, first, size, tail_low, tail_high, row_s, lane_2) * inv
-        physical = jnp.where(kind == 1, 1.0, jnp.where(kind == 2, 0.0, physical))
-        raw = (-DERIVATIVE) * physical * physical * energy
-        spread[pl.ds((first + 1) * ROWS, rows_here), :] = (raw * inv).reshape(rows_here, planes)
-
-    spread_pack_high[...] = spread[strided(ROWS + ROWS - 1), :]
-    spread_pack_low[...] = spread[strided(ROWS), :]
+    def spread_row(r, beyond, next_row, above):
+        density_sum = packed_filter(
+            beyond, packed_row(density, r), packed_row(density, next_row), lane_p, cols_x
+        )
+        modes = []
+        for c in (1, 2, 3):
+            found = corner_modes(packed_nodes(c, r), above(c), lane_p, True)
+            modes.append([mode[:cols_x] for mode in found])
+        result = spread_of(density_sum, modes, passive[strided(r), :], inverse[strided(r), :])
+        spread[strided(ROWS + r), :] = result
+        return result
+
+    spread_pack_low[...] = spread_row(0, row_low[...], 1, lambda c: packed_nodes(c, 1))
+    spread_pack_high[...] = spread_row(
+        ROWS - 1, row_high[0], ROWS - 2, lambda c: row_high[c]
+    )
     for at in (3, 2, 1, 0, 7, 4, 5, 6):
         start_b(at)
 
@@ -422,10 +444,7 @@
         row_c = lax.broadcasted_iota(jnp.int32, shape, 1)
         lane_c = lax.broadcasted_iota(jnp.int32, (count + 2, ROWS, planes), 2)
         wide = spread[pl.ds(first * ROWS, (count + 2) * ROWS), :].reshape(count + 2, ROWS, planes)
-        own, near, far = parts_of_filter(wide, lane_c)
-        side = near[1:-1] + far[:-2] + far[2:]
-        sens = own[1:-1] + near[:-2] + near[2:]
-        sens = sens + (pltpu.roll(side, ROWS - 1, 1) + pltpu.roll(side, 1, 1))
+        sens = plane_filter(wide, lane_c)
         at = pl.ds(first * ROWS, count * ROWS)
         held = big[0, pl.ds((first + 1) * ROWS, count * ROWS), :].reshape(shape)
         sens = middle_rows(sens, row_c)
@@ -463,7 +482,6 @@
 
         lax.fori_loop(0, slots // group, volumes, 0)
 
-    inner = cols_x - 2
     for first in range(1, 1 + inner, size):
         plane_group(first, min(size, 1 + inner - first), first - 1)
     add_volumes(0, inner, True)
@@ -474,20 +492,10 @@
     plane_group(cols_x - 1, 1, inner + 1)
     join(spread_row_high, s_corner_mm[0:1, :], s_corner_pm[0:1, :])
     join(spread_row_low, s_corner_mp[7:8, :], s_corner_pp[7:8, :])
-    lane_p = lax.broadcasted_iota(jnp.int32, (cols_x + ROWS, planes), 1)
-
-    def packed_row(r):
-        above = spread[pl.ds(last + ROWS + r, 1), :]
-        below = spread[pl.ds(r, 1), :]
-        tail = jnp.where(row == 0, above, jnp.where(row == ROWS - 1, below, 0.0))
-        return jnp.concatenate([spread[strided(ROWS + r), :], tail], axis=0)
-
     def edge_row(r, beyond, next_row, held, place):
-        own, near, _ = parts_of_filter(packed_row(r), lane_p)
-        count = own.shape[0]
-        sens = (own + pltpu.roll(near, 1, 0) + pltpu.roll(near, count - 1, 0))[:cols_x]
-        sens = sens + filter_rows(beyond, lane_p, cols_x)
-        sens = sens + filter_rows(packed_row(next_row), lane_p, cols_x)
+        sens = packed_filter(
+            beyond, packed_row(spread, r), packed_row(spread, next_row), lane_p, cols_x
+        )
         rate = rate_of(sens, held, inverse_volume[strided(r), :])
         sens_out[strided(r), :] = sens
         scaled[strided(r), :] = rate
@@ -519,6 +527,9 @@
         ).start()
 
     peers(devices, share)
+    for at in range(8):
+        sent_a(at)
+        sent_b(at)
     others = totals.at[pl.ds(0, devices - 1)]
     pltpu.make_async_copy(others, others, recv_c).wait()
     volume = jnp.sum(totals[...], axis=0)
@@ -534,9 +545,6 @@
         at = pl.ds(first * ROWS, rows_here)
         moved = jnp.maximum(tiles(scaled, first) * factor, tiles(lower, first))
         new_out[at, :] = jnp.minimum(moved, tiles(upper, first)).reshape(rows_here, planes)
-    for at in range(8):
-        sent_a(at)
-        sent_b(at)
     pltpu.make_async_copy(others, others, send_c).wait()
 
 
@@ -583,9 +591,6 @@
             tile,
             tile,
             tile,
-            buffer(3, block + ROWS, planes),
-            field,
-            field,
             field,
             field,
             field,

time: 20.6 us -> 20.4 us (level)
  no operation moved by 1% of the time
where the time goes in v1:
time: 20.4 us; the launch traced here: 20.3 us
  Pallas kernels  19 us (93%)
  local copies, waits for them, and re-layouts  0.66 us (3%)
  between operations  0.64 us (3%)
    pallas_call x1, Pallas kernels, per_device(): pl.pallas_call(functools.partial(kernel, count_x, count_y), out_shape=out...  19 us
    another operation x1, local copies, waits for them, and re-layouts, per_device(): results[1].reshape(density.shape)  0.66 us

profile of v1, /device:TPU:0, one launch (start us, length us, event | category | flops | bytes accessed | tf_op | source)
XLA Modules:
  0.0 20.3 jit_solution(4645931917597282238)
XLA Ops:
  0.6 19.0 %shard_map.50 = f32[2,128,128]{2,1,0:T(8,128)S(1)} custom-call(f32[128,128]{1,0:T(8,128)} %bitcast.8, f32[3,128,128]{2,1,0:T(8,128)} %bitcast.7, s32[128,128]{1,0:T(8,128)} %bitcast.9), custom_call_target="tpu_custom_call" | custom-call | tf_op jit(solution)/shard_map/pallas_call | solution.py:569
  19.6 0.7 %slice_bitcast_fusion = (f32[16,8,128]{2,1,0:T(8,128)}, f32[16,8,128]{2,1,0:T(8,128)}) fusion(f32[2,128,128]{2,1,0:T(8,128)S(1)} %shard_map.50), kind=kLoop, calls=%fused_computation | loop fusion | bytes 262144 | tf_op jit(solution)/shard_map/reshape;squeeze | solution.py:620

commit v2 on v1

--- a/solution.py
+++ b/solution.py
@@ -273,27 +273,6 @@
         send_b,
         recv_b,
     )
-    def strided(start):
-        return pl.ds(start, cols_x, stride=ROWS)
-
-    loads[0].wait()
-    pack_high[...] = big[0, strided(ROWS + ROWS - 1), :]
-    pack_low[0] = big[0, strided(ROWS), :]
-    loads[1].wait()
-    for c in (1, 2, 3):
-        pack_low[c] = big[c, strided(ROWS), :]
-    pl.semaphore_wait(barrier, devices - 1)
-    for at in (3, 1, 2, 7, 0, 4, 5, 6):
-        start_a(at)
-    fill(WAYS[0], [big.at[0, low_tile], spread.at[low_tile]])
-    fill(WAYS[1], [big.at[:, high_tile], spread.at[high_tile]])
-    fill(WAYS[2], [row_low.at[pl.ds(0, cols_x)], spread_row_low.at[pl.ds(0, cols_x)]])
-    fill(WAYS[3], [row_high.at[:, pl.ds(0, cols_x)], spread_row_high.at[pl.ds(0, cols_x)]])
-    fill(WAYS[4], [corner_pp, s_corner_pp])
-    fill(WAYS[5], [corner_mp, s_corner_mp])
-    fill(WAYS[6], [corner_pm, s_corner_pm])
-    fill(WAYS[7], [corner_mm, s_corner_mm])
-
     lane = lax.broadcasted_iota(jnp.int32, (ROWS, planes), 1)
     row = lax.broadcasted_iota(jnp.int32, (ROWS, planes), 0)
 
@@ -341,6 +320,27 @@
                 volume = volume + inverse_sums(x + 1, offset)[1][2]
             weights[key] = 1.0 / volume
         inverse_volume[tile, :] = weights[key]
+
+    def strided(start):
+        return pl.ds(start, cols_x, stride=ROWS)
+
+    loads[0].wait()
+    pack_high[...] = big[0, strided(ROWS + ROWS - 1), :]
+    pack_low[0] = big[0, strided(ROWS), :]
+    loads[1].wait()
+    for c in (1, 2, 3):
+        pack_low[c] = big[c, strided(ROWS), :]
+    pl.semaphore_wait(barrier, devices - 1)
+    for at in (3, 1, 2, 7, 0, 4, 5, 6):
+        start_a(at)
+    fill(WAYS[0], [big.at[0, low_tile], spread.at[low_tile]])
+    fill(WAYS[1], [big.at[:, high_tile], spread.at[high_tile]])
+    fill(WAYS[2], [row_low.at[pl.ds(0, cols_x)], spread_row_low.at[pl.ds(0, cols_x)]])
+    fill(WAYS[3], [row_high.at[:, pl.ds(0, cols_x)], spread_row_high.at[pl.ds(0, cols_x)]])
+    fill(WAYS[4], [corner_pp, s_corner_pp])
+    fill(WAYS[5], [corner_mp, s_corner_mp])
+    fill(WAYS[6], [corner_pm, s_corner_pm])
+    fill(WAYS[7], [corner_mm, s_corner_mm])
 
     size = 4 if cols_x % 4 == 0 else 1
     rows_here = size * ROWS

time: 20.4 us -> 20.4 us (level)
  no operation moved by 1% of the time
where the time goes in v2:
time: 20.4 us; the launch traced here: 20.3 us
  Pallas kernels  19 us (93%)
  local copies, waits for them, and re-layouts  0.66 us (3%)
  between operations  0.64 us (3%)
    pallas_call x1, Pallas kernels, per_device(): pl.pallas_call(functools.partial(kernel, count_x, count_y), out_shape=out...  19 us
    another operation x1, local copies, waits for them, and re-layouts, per_device(): results[1].reshape(density.shape)  0.66 us

profile of v2, /device:TPU:0, one launch (start us, length us, event | category | flops | bytes accessed | tf_op | source)
XLA Modules:
  0.0 20.3 jit_solution(11262402772799925095)
XLA Ops:
  0.6 19.0 %shard_map.50 = f32[2,128,128]{2,1,0:T(8,128)S(1)} custom-call(f32[128,128]{1,0:T(8,128)} %bitcast.8, f32[3,128,128]{2,1,0:T(8,128)} %bitcast.7, s32[128,128]{1,0:T(8,128)} %bitcast.9), custom_call_target="tpu_custom_call" | custom-call | tf_op jit(solution)/shard_map/pallas_call | solution.py:569
  19.6 0.7 %slice_bitcast_fusion = (f32[16,8,128]{2,1,0:T(8,128)}, f32[16,8,128]{2,1,0:T(8,128)}) fusion(f32[2,128,128]{2,1,0:T(8,128)S(1)} %shard_map.50), kind=kLoop, calls=%fused_computation | loop fusion | bytes 262144 | tf_op jit(solution)/shard_map/reshape;squeeze | solution.py:620

commit v3 on v2

--- a/solution.py
+++ b/solution.py
@@ -117,12 +117,23 @@
     return first + second + third
 
 
-def peers(count, body):
-    if count <= 64:
-        for step in range(1, count):
-            body(step)
-    else:
-        lax.fori_loop(1, count, lambda step, carry: (body(step), carry)[1], 0)
+def peers(count_x, count_y, own_column_first, body):
+    count = count_x * count_y
+    if count > 64:
+        pair = lambda step: (step // count_y, step % count_y)
+        lax.fori_loop(1, count, lambda step, carry: (body(*pair(step)), carry)[1], 0)
+        return
+
+    def nearness(step, size):
+        return (min(step, size - step), step)
+
+    columns = sorted(range(1, count_x), key=lambda step: nearness(step, count_x))
+    columns = [0] + columns if own_column_first else columns + [0]
+    rows = sorted(range(count_y), key=lambda step: nearness(step, count_y))
+    for step_x in columns:
+        for step_y in rows:
+            if (step_x, step_y) != (0, 0):
+                body(step_x, step_y)
 
 
 def kernel(
@@ -190,16 +201,16 @@
 
     devices = count_x * count_y
 
-    def peer(step):
-        return (lax.rem(ix + step // count_y, count_x), lax.rem(iy + step % count_y, count_y))
+    def peer(step_x, step_y):
+        return (lax.rem(ix + step_x, count_x), lax.rem(iy + step_y, count_y))
 
     barrier = pltpu.get_barrier_semaphore()
-    peers(
-        devices,
-        lambda step: pl.semaphore_signal(
-            barrier, inc=1, device_id=peer(step), device_id_type=MESH
-        ),
-    )
+    def greet(step_x, step_y):
+        pl.semaphore_signal(
+            barrier, inc=1, device_id=peer(step_x, step_y), device_id_type=MESH
+        )
+
+    peers(count_x, count_y, True, greet)
 
     def fill(way, refs):
         @pl.when(jnp.logical_not(inside(ix - way[0], iy - way[1])))
@@ -427,10 +438,11 @@
         return result
 
     spread_pack_low[...] = spread_row(0, row_low[...], 1, lambda c: packed_nodes(c, 1))
+    start_b(3)
     spread_pack_high[...] = spread_row(
         ROWS - 1, row_high[0], ROWS - 2, lambda c: row_high[c]
     )
-    for at in (3, 2, 1, 0, 7, 4, 5, 6):
+    for at in (2, 1, 0, 7, 4, 5, 6):
         start_b(at)
 
     def rate_of(sens, held, weight):
@@ -516,17 +528,17 @@
             lines = lines + partial[pl.ds(start + s, planes, stride=ROWS), :]
         totals[me, half : half + 1, :] = jnp.sum(lines.T, axis=0, keepdims=True)
 
-    def share(step):
+    def share(step_x, step_y):
         pltpu.make_async_remote_copy(
             src_ref=totals.at[me],
             dst_ref=totals.at[me],
             send_sem=send_c,
             recv_sem=recv_c,
-            device_id=peer(step),
+            device_id=peer(step_x, step_y),
             device_id_type=MESH,
         ).start()
 
-    peers(devices, share)
+    peers(count_x, count_y, False, share)
     for at in range(8):
         sent_a(at)
         sent_b(at)

time: 20.4 us -> 20.6 us (level)
  no operation moved by 1% of the time
where the time goes in v3:
time: 20.6 us; the launch traced here: 20.4 us
  Pallas kernels  19.1 us (93%)
  local copies, waits for them, and re-layouts  0.66 us (3%)
  between operations  0.64 us (3%)
    pallas_call x1, Pallas kernels, per_device(): pl.pallas_call(functools.partial(kernel, count_x, count_y), out_shape=out...  19.1 us
    another operation x1, local copies, waits for them, and re-layouts, per_device(): results[1].reshape(density.shape)  0.66 us

profile of v3, /device:TPU:0, one launch (start us, length us, event | category | flops | bytes accessed | tf_op | source)
XLA Modules:
  0.0 20.4 jit_solution(8966425465018539726)
XLA Ops:
  0.6 19.1 %shard_map.50 = f32[2,128,128]{2,1,0:T(8,128)S(1)} custom-call(f32[128,128]{1,0:T(8,128)} %bitcast.8, f32[3,128,128]{2,1,0:T(8,128)} %bitcast.7, s32[128,128]{1,0:T(8,128)} %bitcast.9), custom_call_target="tpu_custom_call" | custom-call | tf_op jit(solution)/shard_map/pallas_call | solution.py:581
  19.8 0.7 %slice_bitcast_fusion = (f32[16,8,128]{2,1,0:T(8,128)}, f32[16,8,128]{2,1,0:T(8,128)}) fusion(f32[2,128,128]{2,1,0:T(8,128)S(1)} %shard_map.50), kind=kLoop, calls=%fused_computation | loop fusion | bytes 262144 | tf_op jit(solution)/shard_map/reshape;squeeze | solution.py:632
